TPU v7x, 512 devices: a whole 4x4x16 slice. The times are simulated.
512 devices in a mesh: rows: 128 (over z, x, core), tower: 4 (over y).
Axes of the slice: x: 4, y: 4, z: 16, core: 2. Of those that a mesh axis runs over, the one named last changes fastest.
Arguments:
- pool_img: bfloat16 [65536, 1024], P('rows'), may hold values from -6 to 6
- pool_txt: bfloat16 [65536, 1024], P('rows'), may hold values from -6 to 6
- w_img: bfloat16 [1024, 512], P(None, 'tower'), may hold values from -1 to 1
- w_txt: bfloat16 [1024, 512], P(None, 'tower'), may hold values from -1 to 1
- logit_scale: float32 [1], replicated, may hold values from 16 to 40
- logit_bias: float32 [1], replicated, may hold values from -10 to -6
- loss_scale: float32 [1], replicated, may hold values from 256 to 1024
- select: int32 [32768], P('rows'), may hold values from 0 to 511, as said below
- counts: int32 [128], P('rows'), may hold values from 0 to 256, as said below
Outputs:
- grad_w_img: float32 [1024, 512], P('rows', 'tower')
- grad_w_txt: float32 [1024, 512], P('rows', 'tower')
Inputs may be any that keep to these rules, and one draw needn't show every extreme that they name: `select`: each device's list names distinct rows of its own 512 super-batch rows. The counts of all devices sum to 16384; some device's count is 256.
All inputs are finite; a program needn't handle non-finite values.
Results may differ from a plain program's by a relative error of at most 0.0013.
Values may be sent and summed in bfloat16 or wider, within the bound.
A program may use at most 64 MiB of HBM per device.

v0:
```python
import jax
import jax.numpy as jnp
from jax import lax
from jax.sharding import PartitionSpec as P

LRN = 128


eps = 1e-06


def entering(shard, axis, combine, identity):
    size, here = (lax.axis_size(axis), lax.axis_index(axis))
    everything = lax.all_gather(shard, axis)
    start = jnp.broadcast_to(jnp.asarray(identity, shard.dtype), shard.shape)

    def lap(k, before):
        reached = k < here
        new = combine(before, everything[k])
        return jnp.where(reached, new, before)

    return lax.fori_loop(0, size, lap, start)


def project_rows(feats, weight):
    proj = jnp.dot(feats, weight, preferred_element_type=jnp.float32)
    return (proj, jnp.sum(proj * proj, axis=1))


def add_counts(earlier, later):
    return earlier + later


def pair_terms(
    rows_emb, shard_piece, row_ids, quarter, learn_rows, first_row, temper_val, bias_val
):
    col_index = jnp.arange(shard_piece.shape[0], dtype=jnp.int32)
    col_ids = col_index // quarter * learn_rows + first_row + col_index % quarter
    logits = (
        temper_val
        * lax.dot_general(
            rows_emb, shard_piece, (((1,), (1,)), ((), ())), preferred_element_type=jnp.float32
        )
        + bias_val
    )
    labels = (row_ids[:, None] == col_ids[None, :]).astype(jnp.float32)
    weights = (jax.nn.sigmoid(logits) - labels).astype(jnp.bfloat16)
    return jnp.dot(weights, shard_piece, preferred_element_type=jnp.float32)


def on_device(
    pool_img, pool_txt, w_img, w_txt, logit_scale, logit_bias, loss_scale, select, counts
):
    rows_n = lax.axis_size("rows")
    tower_n = lax.axis_size("tower")
    row_at = lax.axis_index("rows")
    tower_at = lax.axis_index("tower")
    list_len = select.shape[0]
    per_peer = (list_len + rows_n - 1) // rows_n
    learn_rows = LRN
    quarter = learn_rows // tower_n
    temper_val = logit_scale[0]
    bias_val = logit_bias[0]
    list_index = jnp.arange(list_len, dtype=jnp.int32)
    is_live = list_index < counts[0]
    offsets = entering(counts, "rows", add_counts, jnp.zeros((1,), jnp.int32))
    dest = (offsets[0] + list_index) % rows_n
    feats_img = jnp.take(pool_img, select, axis=0)
    feats_txt = jnp.take(pool_txt, select, axis=0)
    proj_img, square_img = project_rows(feats_img, w_img)
    proj_txt, square_txt = project_rows(feats_txt, w_txt)
    square_img, square_txt = lax.psum((square_img, square_txt), "tower")
    norm_img = lax.rsqrt(square_img + eps)
    norm_txt = lax.rsqrt(square_txt + eps)
    unit_img = proj_img * norm_img[:, None]
    unit_txt = proj_txt * norm_txt[:, None]
    dest_hits = (
        (dest[:, None] == jnp.arange(rows_n, dtype=jnp.int32)[None, :]) & is_live[:, None]
    ).astype(jnp.int32)
    within = jnp.sum((jnp.cumsum(dest_hits, axis=0) - 1) * dest_hits, axis=1)
    outgoing = jnp.where(is_live, dest * per_peer + within, rows_n * per_peer)
    placing = (outgoing[None, :] == jnp.arange(rows_n * per_peer, dtype=jnp.int32)[:, None]).astype(
        jnp.bfloat16
    )
    sent_img = jnp.dot(
        placing, unit_img.astype(jnp.bfloat16), preferred_element_type=jnp.float32
    ).astype(jnp.bfloat16)
    sent_txt = jnp.dot(
        placing, unit_txt.astype(jnp.bfloat16), preferred_element_type=jnp.float32
    ).astype(jnp.bfloat16)
    slot_flags = jnp.sum(placing.astype(jnp.float32), axis=1).astype(jnp.bfloat16)
    got_img, got_txt, got_flag = (
        lax.all_to_all(sent_img, "rows", split_axis=0, concat_axis=0, tiled=True),
        lax.all_to_all(sent_txt, "rows", split_axis=0, concat_axis=0, tiled=True),
        lax.all_to_all(slot_flags, "rows", split_axis=0, concat_axis=0, tiled=True),
    )
    arrived = got_flag > 0.5
    arrive_rank = jnp.cumsum(arrived.astype(jnp.int32)) - 1
    gather_rows = (
        (arrive_rank[None, :] == jnp.arange(learn_rows, dtype=jnp.int32)[:, None])
        & arrived[None, :]
    ).astype(jnp.bfloat16)
    own_img = jnp.dot(gather_rows, got_img, preferred_element_type=jnp.float32).astype(jnp.bfloat16)
    own_txt = jnp.dot(gather_rows, got_txt, preferred_element_type=jnp.float32).astype(jnp.bfloat16)
    full_img, full_txt = (
        lax.all_gather(own_img, "tower", axis=1, tiled=True),
        lax.all_gather(own_txt, "tower", axis=1, tiled=True),
    )
    first_row = tower_at * quarter
    part_img = lax.dynamic_slice_in_dim(full_img, first_row, quarter, 0)
    part_txt = lax.dynamic_slice_in_dim(full_txt, first_row, quarter, 0)
    row_ids = row_at * learn_rows + jnp.arange(learn_rows, dtype=jnp.int32)
    side_img = pair_terms(
        full_img,
        lax.all_gather(part_txt, "rows", axis=0, tiled=True),
        row_ids,
        quarter,
        learn_rows,
        first_row,
        temper_val,
        bias_val,
    )
    side_txt = pair_terms(
        full_txt,
        lax.all_gather(part_img, "rows", axis=0, tiled=True),
        row_ids,
        quarter,
        learn_rows,
        first_row,
        temper_val,
        bias_val,
    )
    summed_img, summed_txt = (
        lax.psum_scatter(side_img, "tower", scatter_dimension=1, tiled=True),
        lax.psum_scatter(side_txt, "tower", scatter_dimension=1, tiled=True),
    )
    factor = loss_scale[0] * temper_val / (learn_rows * rows_n)
    back_rank = jnp.clip(arrive_rank, 0, learn_rows - 1)
    arrive_mask = arrived.astype(jnp.float32)[:, None]
    back_img = jnp.take(factor * summed_img, back_rank, axis=0) * arrive_mask
    back_txt = jnp.take(factor * summed_txt, back_rank, axis=0) * arrive_mask
    ret_img, ret_txt = (
        lax.all_to_all(back_img, "rows", split_axis=0, concat_axis=0, tiled=True),
        lax.all_to_all(back_txt, "rows", split_axis=0, concat_axis=0, tiled=True),
    )
    home_slot = jnp.clip(outgoing, 0, rows_n * per_peer - 1)
    keep_mask = is_live.astype(jnp.float32)[:, None]
    grad_unit_img = jnp.take(ret_img, home_slot, axis=0) * keep_mask
    grad_unit_txt = jnp.take(ret_txt, home_slot, axis=0) * keep_mask
    inner_img, inner_txt = lax.psum(
        (jnp.sum(unit_img * grad_unit_img, axis=1), jnp.sum(unit_txt * grad_unit_txt, axis=1)),
        "tower",
    )
    grad_proj_img = (norm_img[:, None] * (grad_unit_img - unit_img * inner_img[:, None])).astype(
        jnp.bfloat16
    )
    grad_proj_txt = (norm_txt[:, None] * (grad_unit_txt - unit_txt * inner_txt[:, None])).astype(
        jnp.bfloat16
    )
    feat_block = feats_img
    grad_w_img = lax.psum_scatter(
        lax.dot_general(
            feat_block, grad_proj_img, (((0,), (0,)), ((), ())), preferred_element_type=jnp.float32
        ),
        "rows",
        scatter_dimension=0,
        tiled=True,
    )
    feat_block = feats_txt
    grad_w_txt = lax.psum_scatter(
        lax.dot_general(
            feat_block, grad_proj_txt, (((0,), (0,)), ((), ())), preferred_element_type=jnp.float32
        ),
        "rows",
        scatter_dimension=0,
        tiled=True,
    )
    return (grad_w_img, grad_w_txt)


def solution(mesh):
    in_specs = (
        P("rows", None),
        P("rows", None),
        P(None, "tower"),
        P(None, "tower"),
        P(),
        P(),
        P(),
        P("rows"),
        P("rows"),
    )
    out_specs = (P("rows", "tower"), P("rows", "tower"))
    return jax.shard_map(
        on_device, mesh=mesh, in_specs=in_specs, out_specs=out_specs, check_vma=False
    )
```

profile of v0, /device:TPU:1, one launch (start us, length us, event | category | flops | bytes accessed | tf_op | source)
XLA Modules:
  0.0 1009.8 jit_solution(7395093799051263732)
XLA Ops:
  7.9 1.4 fusion.82
  10.2 30.3 %all-reduce = s32[128]{0:T(128)S(1)} all-reduce(s32[128]{0:T(128)S(1)} %dynamic-update-slice), channel_id=2, replica_groups=mesh['rows'=128,'tower'=4] {'rows'}, use_global_device_ids=true, to_apply=%add | all-reduce | flops 128 | bytes 1024
  40.4 158.9 %while.13 = (s32[]{:T(128)}, s32[1]{0:T(128)}, s32[]{:T(128)}, s32[128,1]{0,1:T(1,128)S(1)}, s32[]{:T(128)}) while((s32[]{:T(128)}, s32[1]{0:T(128)}, s32[]{:T(128)}, s32[128,1]{0,1:T(1,128)S(1)}, s32[]{:T(128)}) %tuple.57), condition=%wide.region_3.5_spmd, body=%wide.region_2.4_spmd.sunk | while | flops 5 | bytes 107 | solution.py:22
  201.1 13.3 %all-to-all-start = ((bf16[128,2,1]{1,2,0:T(2,128)(2,1)}), bf16[128,2,1]{1,2,0:T(2,128)(2,1)S(1)}, u32[]{:S(2)}, u32[]{:S(2)}) async-start(bf16[128,2,1]{1,2,0:T(2,128)(2,1)} %all_to_all.52), calls=%async_computation | async-start | bytes 131072 | tf_op jit(solution)/shard_map/all_to_all | solution.py:95
  218.2 1.4 multiply_reduce_fusion.2
  219.5 1.4 multiply_reduce_fusion.3
  220.9 9.0 all-reduce.5
  230.8 17.8 %all-to-all-start.2 = ((bf16[128,2,128]{2,1,0:T(2,128)(2,1)}), bf16[128,2,128]{2,1,0:T(2,128)(2,1)S(1)}, u32[]{:S(2)}, u32[]{:S(2)}) async-start(bf16[128,2,128]{2,1,0:T(2,128)(2,1)} %bitcast.14), calls=%async_computation.2 | async-start | bytes 131072 | tf_op jit(solution)/shard_map/all_to_all | solution.py:94
  250.0 13.4 %all-to-all-done.2 = bf16[128,2,128]{2,1,0:T(2,128)(2,1)S(1)} async-done(((bf16[128,2,128]{2,1,0:T(2,128)(2,1)}), bf16[128,2,128]{2,1,0:T(2,128)(2,1)S(1)}, u32[]{:S(2)}, u32[]{:S(2)}) %all-to-all-start.2) | async-done | bytes 65568 | tf_op jit(solution)/shard_map/all_to_all | solution.py:94
  263.6 8.4 all_gather.21
  272.8 22.8 %all_to_all.58 = bf16[128,2,128]{2,1,0:T(2,128)(2,1)S(1)} all-to-all(bf16[128,2,128]{2,1,0:T(2,128)(2,1)S(1)} %bitcast.56), channel_id=1, replica_groups=mesh['rows'=128,'tower'=4] {'rows'}, dimensions={0} | all-to-all | bytes 131072 | tf_op jit(solution)/shard_map/all_to_all | solution.py:93
  295.7 8.8 all_gather.20
  307.4 99.9 %all-gather.4.cloned.1.call-done = bf16[4096,512]{1,0:T(8,128)(2,1)} async-done(((bf16[32,512]{1,0:T(8,128)(2,1)}), bf16[4096,512]{1,0:T(8,128)(2,1)}) %all-gather.4.cloned.1.call-update) | async-done | bytes 4194320 | tf_op jit(solution)/shard_map/all_gather | solution.py:115
  407.3 6.3 fusion.15
  413.6 134.8 %all-gather.6.cloned.1.call-done = bf16[4096,512]{1,0:T(8,128)(2,1)} async-done(((bf16[32,512]{1,0:T(8,128)(2,1)}), bf16[4096,512]{1,0:T(8,128)(2,1)}) %all-gather.6.cloned.1.call-update) | async-done | bytes 4194320 | tf_op jit(solution)/shard_map/all_gather | solution.py:125
  548.4 6.3 fusion.14
  554.7 18.1 %reduce-scatter.3.cloned.1.call-done = f32[128,128]{1,0:T(8,128)} async-done(((f32[128,512]{1,0:T(8,128)}), f32[128,128]{1,0:T(8,128)}) %reduce-scatter.3.cloned.1.call-update) | async-done | bytes 65552 | tf_op jit(solution)/shard_map/reduce_scatter | solution.py:134
  574.4 29.4 %reduce-scatter.5.cloned.1.call-done = f32[128,128]{1,0:T(8,128)} async-done(((f32[128,512]{1,0:T(8,128)}), f32[128,128]{1,0:T(8,128)}) %reduce-scatter.5.cloned.1.call-update) | async-done | bytes 65552 | tf_op jit(solution)/shard_map/reduce_scatter | solution.py:135
  606.1 35.0 %all_to_all.59 = f32[128,2,128]{2,1,0:T(2,128)S(1)} all-to-all(f32[128,2,128]{2,1,0:T(2,128)S(1)} %bitcast.55), channel_id=1, replica_groups=mesh['rows'=128,'tower'=4] {'rows'}, dimensions={0} | all-to-all | bytes 262144 | tf_op jit(solution)/shard_map/all_to_all | solution.py:144
  641.2 6.8 all-to-all-start.3
  648.9 15.1 %all-to-all-done.3 = f32[128,2,128]{2,1,0:T(2,128)S(1)} async-done(((f32[128,2,128]{2,1,0:T(2,128)}), f32[128,2,128]{2,1,0:T(2,128)S(1)}, u32[]{:S(2)}, u32[]{:S(2)}) %all-to-all-start.3) | async-done | bytes 131104 | tf_op jit(solution)/shard_map/all_to_all | solution.py:143
  665.0 6.6 all-reduce.4
  672.8 1.3 fusion.27
  674.7 326.1 %all-reduce.8.cloned.1.call-done = (f32[1024,128]{1,0:T(8,128)}, f32[1024,128]{1,0:T(8,128)}) async-done(((f32[1024,128]{1,0:T(8,128)}, f32[1024,128]{1,0:T(8,128)}), (f32[1024,128]{1,0:T(8,128)}, f32[1024,128]{1,0:T(8,128)})) %all-reduce.8.cloned.1.call-update) | async-done | bytes 1048592
  (201 shorter events, 96.3 us)
Async XLA Ops:
  7.2 208.6 %copy-start = (bf16[512,1024]{1,0:T(8,128)(2,1)S(1)}, bf16[512,1024]{1,0:T(8,128)(2,1)}, u32[]{:S(2)}) copy-start(bf16[512,1024]{1,0:T(8,128)(2,1)} %param.18) | copy-start | bytes 3145732
  201.1 29.7 %all-to-all-start = ((bf16[128,2,1]{1,2,0:T(2,128)(2,1)}), bf16[128,2,1]{1,2,0:T(2,128)(2,1)S(1)}, u32[]{:S(2)}, u32[]{:S(2)}) async-start(bf16[128,2,1]{1,2,0:T(2,128)(2,1)} %all_to_all.52), calls=%async_computation | async-start | bytes 131072 | tf_op jit(solution)/shard_map/all_to_all | solution.py:95
  215.8 1.2 copy-start.1
  230.8 32.7 %all-to-all-start.2 = ((bf16[128,2,128]{2,1,0:T(2,128)(2,1)}), bf16[128,2,128]{2,1,0:T(2,128)(2,1)S(1)}, u32[]{:S(2)}, u32[]{:S(2)}) async-start(bf16[128,2,128]{2,1,0:T(2,128)(2,1)} %bitcast.14), calls=%async_computation.2 | async-start | bytes 131072 | tf_op jit(solution)/shard_map/all_to_all | solution.py:94
  248.6 158.7 %all-gather.4.cloned.1.call-start = ((), (), s32[]{:S(2)}) async-start(), calls=%async_computation.7 | async-start | bytes 4227072 | tf_op jit(solution)/shard_map/all_gather | solution.py:115
  272.6 275.8 %all-gather.6.cloned.1.call-start = ((), (), s32[]{:S(2)}) async-start(), calls=%async_computation.9 | async-start | bytes 4227072 | tf_op jit(solution)/shard_map/all_gather | solution.py:125
  305.1 267.6 %reduce-scatter.3.cloned.1.call-start = ((), (), s32[]{:S(2)}) async-start(), calls=%async_computation.8 | async-start | bytes 327680 | tf_op jit(solution)/shard_map/reduce_scatter | solution.py:134
  413.6 190.2 %reduce-scatter.5.cloned.1.call-start = ((), (), s32[]{:S(2)}) async-start(), calls=%async_computation.10 | async-start | bytes 327680 | tf_op jit(solution)/shard_map/reduce_scatter | solution.py:135
  641.2 22.9 %all-to-all-start.3 = ((f32[128,2,128]{2,1,0:T(2,128)}), f32[128,2,128]{2,1,0:T(2,128)S(1)}, u32[]{:S(2)}, u32[]{:S(2)}) async-start(f32[128,2,128]{2,1,0:T(2,128)} %bitcast.17), calls=%async_computation.4 | async-start | bytes 262144 | tf_op jit(solution)/shard_map/all_to_all | solution.py:143
  648.0 352.8 %all-reduce.8.cloned.1.call-start = ((), (), s32[]{:S(2)}) async-start(), calls=%async_computation.11 | async-start | bytes 2097152
Sparse Core Ops, SparseCore 0:
  272.7 134.5 all-gather.3
  410.4 137.9 all-gather.5
  551.2 21.5 reduce-scatter.2
  575.7 28.0 reduce-scatter.4
  674.2 326.5 all-reduce.7
where the time goes:
time: 1020 us; the launch traced here: 1010 us
  waiting for transfers between devices  637 us (62%)
  blocking collectives  121 us (12%)
  local copies, waits for them, and re-layouts  89 us (9%)
  loops' own time  82.7 us (8%)
  starting transfers between devices  38.4 us (4%)
  matrix products  19.1 us (2%)
  between operations  17.3 us (2%)
    unnamed x6, waiting for transfers between devices  326 us
    all_gather x1, waiting for transfers between devices, on_device(): lax.all_gather(part_img, 'rows', axis=0, tiled=True)  135 us
    all_gather x1, waiting for transfers between devices, on_device(): lax.all_gather(part_txt, 'rows', axis=0, tiled=True)  99.9 us
    another operation x1, loops' own time, entering(): return lax.fori_loop(0, size, lap, start)  82.7 us
    dynamic_slice x128, local copies, waits for them, and re-layouts, lap(): new = combine(before, everything[k])  76.2 us
    all_to_all x1, blocking collectives, on_device(): lax.all_to_all(back_txt, 'rows', split_axis=0, concat_axis=0, tiled=True)  35 us
    unnamed x1, blocking collectives  30.3 us
    reduce_scatter x1, waiting for transfers between devices, on_device(): lax.psum_scatter(side_txt, 'tower', scatter_dimension=1, tiled=True)  29.4 us
  transfers between devices with their start and end apart: 8, of which 7 were waited for; matrix products, arithmetic and copies ran while one was open for 2% of the time, Pallas kernels for 0%

commit v1 on v0

v1 whole, which is shorter than its diff:
```python
import functools

import jax
import jax.numpy as jnp
from jax import lax
from jax.experimental import pallas as pl
from jax.experimental.pallas import tpu as pltpu
from jax.sharding import PartitionSpec as P

bf16 = jnp.bfloat16
f32 = jnp.float32
eps = 1e-06

NX, NC = 4, 2
LRN = 128
GROUP, TILE = 4, 4
ZCH = 2


def dot(a, b, ca=1, cb=0):
    return lax.dot_general(a, b, (((ca,), (cb,)), ((), ())), preferred_element_type=f32)


def chip_order(nx, ny):
    ring = lambda d, n: min(d, n - d)
    places = [(dx, dy) for dx in range(nx) for dy in range(ny)]
    return sorted(places, key=lambda p: (ring(p[0], nx) + ring(p[1], ny), p))


def kernel(
    cfg,
    pool_img, pool_txt, w_img, w_txt, sel, cnt, temper, bias, loss_scale,
    out_img, out_txt,
    feats, proj, unit, norm, zbuf, pbuf, gimg, gtxt, rz_up, rz_dn, rcore, sbuf, rxy,
    gp, gpr, gw, gwc, gx, gxr, gz, gzr,
    y_sem, za_up, za_dn, xy_sem, cf_sem, zr_up, zr_dn, cr_sem, xr_sem, yb_sem,
    fc_sem, fx_sem, fz_sem,
):
    nz, ny, chips = cfg
    row, y = lax.axis_index("rows"), lax.axis_index("tower")
    c = row % NC
    x = row // NC % NX
    z = row // (NC * NX)
    half = nz // 2
    order = chip_order(NX, ny)
    groups, tiles = nz // GROUP, len(order) // TILE
    slots = unit.shape[2]
    emb_w = zbuf.shape[2]
    col_w = proj.shape[2]
    sends = []

    def at(dz=0, dx=0, dy=0, dc=0):
        r = ((z + dz + nz) % nz * NX + (x + dx + NX) % NX) * NC + (c + dc) % NC
        return (r, (y + dy + ny) % ny)

    def send(src, dst, sems, where):
        copy = pltpu.make_async_remote_copy(
            src_ref=src, dst_ref=dst, send_sem=sems.at[0], recv_sem=sems.at[1],
            device_id=where, device_id_type=pl.DeviceIdType.MESH,
        )
        copy.start()
        sends.append(copy)

    def arrived(ref, sems):
        pltpu.make_async_remote_copy(
            src_ref=ref, dst_ref=ref, send_sem=sems.at[0], recv_sem=sems.at[1],
            device_id=at(), device_id_type=pl.DeviceIdType.MESH,
        ).wait_recv()

    partners = [at(dx=dx, dy=dy) for dx, dy in order[1:]]
    partners += [at(dz=dz) for dz in range(1, nz)] + [at(dc=1)]
    barrier = pltpu.get_barrier_semaphore()
    for there in partners:
        pl.semaphore_signal(
            barrier, inc=1, device_id=there, device_id_type=pl.DeviceIdType.MESH
        )

    pool_rows = pool_img.shape[0]
    cols = lax.broadcasted_iota(jnp.int32, (sel.shape[0], pool_rows), 1)
    pick = jnp.where(sel[...] == cols, 1.0, 0.0).astype(bf16)
    for side, (pool, w) in enumerate(((pool_img, w_img), (pool_txt, w_txt))):
        feats[side] = dot(pick, pool[...]).astype(bf16)
        proj[side] = dot(feats[side], w[...])
    pl.semaphore_wait(barrier, len(partners))

    for dy in range(1, ny):
        yy = (y + dy) % ny
        send(
            proj.at[:, pl.ds(pl.multiple_of(yy * slots, slots), slots)],
            unit.at[y], y_sem.at[dy - 1], at(dy=dy),
        )
    unit[y] = proj[:, pl.ds(pl.multiple_of(y * slots, slots), slots)]
    for dy in range(1, ny):
        arrived(unit.at[(y - dy + ny) % ny], y_sem.at[dy - 1])
    slot_at = y * slots + lax.broadcasted_iota(jnp.int32, (slots, 1), 0)
    live = slot_at < cnt[0]
    for side in range(2):
        square = sum(
            jnp.sum(unit[k, side] * unit[k, side], axis=1, keepdims=True) for k in range(ny)
        )
        norm[side] = lax.rsqrt(square + eps)
        for k in range(ny):
            unit[k, side] = unit[k, side] * norm[side]
            emb = jnp.where(live, unit[k, side], 0.0).astype(bf16)
            if side == 0:
                zbuf[0, :, k * col_w:(k + 1) * col_w] = emb
            else:
                pbuf[0, 0, :, k * col_w:(k + 1) * col_w] = emb

    def spot(offset):
        return 2 * offset if offset >= 0 else -2 * offset - 1

    zrows = slots // ZCH

    def ring_send(s):
        for h in range(ZCH):
            rows = pl.ds(h * zrows, zrows)
            if s > 1:
                arrived(zbuf.at[spot(1 - s), rows], za_up.at[s - 2, h])
            if s <= half:
                send(zbuf.at[spot(1 - s), rows], zbuf.at[spot(-s), rows],
                     za_up.at[s - 1, h], at(dz=1))
            if 1 < s <= nz - half:
                arrived(zbuf.at[spot(s - 1), rows], za_dn.at[s - 2, h])
            if s < nz - half:
                send(zbuf.at[spot(s - 1), rows], zbuf.at[spot(s), rows],
                     za_dn.at[s - 1, h], at(dz=-1))

    def hand_over(t):
        for n in range(t * TILE, (t + 1) * TILE):
            if n:
                arrived(pbuf.at[n, 0], xy_sem.at[n - 1])
                send(pbuf.at[n, 0], pbuf.at[n, 1], cf_sem.at[n], at(dc=1))

    def tile_ready(t):
        for n in range(t * TILE, (t + 1) * TILE):
            arrived(pbuf.at[n, 1], cf_sem.at[n])

    def pair_tile(g, t):
        img = zbuf[g * GROUP:(g + 1) * GROUP].reshape(GROUP * slots, emb_w)
        txt = pbuf[t * TILE:(t + 1) * TILE].reshape(TILE * NC * slots, emb_w)
        logits = temper[0] * dot(img, txt, 1, 1) + bias[0]
        weights = 1.0 / (1.0 + jnp.exp(-logits))
        if g == 0 and t == 0:
            i = lax.broadcasted_iota(jnp.int32, logits.shape, 0)
            j = lax.broadcasted_iota(jnp.int32, logits.shape, 1)
            weights = jnp.where((i == j) & (i < slots), 0.0, weights)
        weights = weights.astype(bf16)
        to_img = dot(weights, txt).reshape(GROUP, slots, emb_w)
        to_txt = dot(weights, img, 0, 0).reshape(TILE, NC, slots, emb_w)
        at_img = slice(g * GROUP, (g + 1) * GROUP)
        at_txt = slice(t * TILE, (t + 1) * TILE)
        gimg[at_img] = to_img if (g, t) in first_img else gimg[at_img] + to_img
        gtxt[at_txt] = to_txt if (g, t) in first_txt else gtxt[at_txt] + to_txt

    phases = []
    for k in range(groups):
        if k < groups - 1:
            phases.append([(k, t) for t in range(k)] + [(g, k) for g in range(k + 1)])
        else:
            phases.append([(k, t) for t in range(tiles)]
                          + [(g, k) for g in range(k - 1, -1, -1)])
    flat = [p for phase in phases for p in phase]
    first_img = {next(p for p in flat if p[0] == g) for g in range(groups)}
    first_txt = {next(p for p in flat if p[1] == t) for t in range(tiles)}

    queue = []
    opened = 0
    for s in range(1, half + 2):
        ring_send(s)
        if s == 1:
            send(pbuf.at[0, 0], pbuf.at[0, 1], cf_sem.at[0], at(dc=1))
            for n, (dx, dy) in enumerate(order[1:]):
                send(pbuf.at[0, 0], pbuf.at[n + 1, 0], xy_sem.at[n], at(dx=dx, dy=dy))
        if (s - 1) * 2 >= (opened + 1) * GROUP:
            tile_ready(opened)
            queue += phases[opened]
            opened += 1
        if s <= half:
            for p in queue[:2]:
                pair_tile(*p)
            queue = queue[2:]
        if opened < tiles and s * 2 >= (opened + 1) * GROUP:
            hand_over(opened)
    early = [p for p in queue if p[0] < groups - 1 and p[1] < tiles - 1]
    last = [p for p in queue if p[0] == groups - 1]
    rest = [p for p in queue if p[0] < groups - 1 and p[1] == tiles - 1]
    for p in early + last:
        pair_tile(*p)

    def ring_sum(s):
        for h in range(ZCH):
            rows = pl.ds(h * zrows, zrows)
            if s <= half:
                k = spot(half + 1 - s) if s > 1 else spot(-half)
                if s > 1:
                    arrived(rz_up.at[s - 2, rows], zr_up.at[s - 2, h])
                    gimg[k, rows] = gimg[k, rows] + rz_up[s - 2, rows]
                send(gimg.at[k, rows], rz_up.at[s - 1, rows], zr_up.at[s - 1, h], at(dz=1))
            if s < nz - half:
                k = spot(s - (nz - half))
                if s > 1:
                    arrived(rz_dn.at[s - 2, rows], zr_dn.at[s - 2, h])
                    gimg[k, rows] = gimg[k, rows] + rz_dn[s - 2, rows]
                send(gimg.at[k, rows], rz_dn.at[s - 1, rows], zr_dn.at[s - 1, h], at(dz=-1))

    def core_send():
        for t in range(tiles):
            part = pl.ds(t * TILE, TILE)
            send(gtxt.at[part, 1], rcore.at[part], cr_sem.at[t], at(dc=1))

    def plane_send(t):
        part = pl.ds(t * TILE, TILE)
        arrived(rcore.at[part], cr_sem.at[t])
        for n in range(t * TILE, (t + 1) * TILE):
            both = gtxt[n, 0] + rcore[n]
            if n == 0:
                gtxt[0, 0] = both
            else:
                sbuf[n] = both.astype(sbuf.dtype)
                dx, dy = order[n]
                send(sbuf.at[n], rxy.at[n], xr_sem.at[n - 1], at(dx=-dx, dy=-dy))

    ring_sum(1)
    for p in rest:
        pair_tile(*p)
    core_send()
    for s in range(2, half + 1):
        ring_sum(s)
        if s - 2 < tiles:
            plane_send(s - 2)
    for t in range(max(half - 1, 0), tiles):
        plane_send(t)

    emb_i = zbuf[0].astype(f32)
    emb_t = pbuf[0, 0].astype(f32)
    own = temper[0] * jnp.sum(emb_i * emb_t, axis=1, keepdims=True) + bias[0]
    own = (-1.0 / (1.0 + jnp.exp(own))).astype(bf16).astype(f32)
    factor = loss_scale[0] * temper[0] / (LRN * nz * NX * NC)

    def finish(side, total, other):
        grad = jnp.where(live, factor * (total + own * other), 0.0)
        inner = sum(
            jnp.sum(unit[k, side] * grad[:, k * col_w:(k + 1) * col_w], axis=1, keepdims=True)
            for k in range(ny)
        )
        for k in range(ny):
            part = grad[:, k * col_w:(k + 1) * col_w]
            gp[k, side] = (norm[side] * (part - unit[k, side] * inner)).astype(bf16)

    for n in range(1, len(order)):
        arrived(rxy.at[n], xr_sem.at[n - 1])
    total = gtxt[0, 0]
    for n in range(1, len(order)):
        total = total + rxy[n].astype(f32)
    finish(1, total, emb_i)
    total = gimg[0]
    for h in range(ZCH):
        rows = pl.ds(h * zrows, zrows)
        arrived(rz_up.at[half - 1, rows], zr_up.at[half - 1, h])
        if nz - half > 1:
            arrived(rz_dn.at[nz - half - 2, rows], zr_dn.at[nz - half - 2, h])
    total = total + rz_up[half - 1]
    if nz - half > 1:
        total = total + rz_dn[nz - half - 2]
    finish(0, total, emb_t)

    for dy in range(1, ny):
        send(gp.at[(y + dy) % ny], gpr.at[y], yb_sem.at[dy - 1], at(dy=dy))
    gpr[y] = gp[y]
    for dy in range(1, ny):
        arrived(gpr.at[(y - dy + ny) % ny], yb_sem.at[dy - 1])
    for side in range(2):
        grad = gpr[:, side].reshape(ny * slots, col_w)
        gw[side] = dot(feats[side], grad, 0, 0).reshape(gw.shape[1:])

    send(gw.at[:, :, :, 1 - c], gwc, fc_sem, at(dc=1))
    arrived(gwc, fc_sem)
    gx[...] = gw[:, :, :, c] + gwc[...]
    for dx in range(1, NX):
        send(gx.at[:, :, (x + dx) % NX], gxr.at[dx - 1], fx_sem.at[dx - 1], at(dx=dx))
    total = gx[:, :, x]
    for dx in range(1, NX):
        arrived(gxr.at[dx - 1], fx_sem.at[dx - 1])
        total = total + gxr[dx - 1]
    gz[...] = total
    for dz in range(1, nz):
        send(gz.at[:, (z + dz) % nz], gzr.at[dz - 1], fz_sem.at[dz - 1], at(dz=dz))
    total = gz[:, z]
    for dz in range(1, nz):
        arrived(gzr.at[dz - 1], fz_sem.at[dz - 1])
        total = total + gzr[dz - 1]
    out_img[...] = total[0]
    out_txt[...] = total[1]
    for copy in sends:
        copy.wait_send()


def on_device(
    pool_img, pool_txt, w_img, w_txt, logit_scale, logit_bias, loss_scale, select, counts
):
    ny = lax.axis_size("tower")
    rows_n = lax.axis_size("rows")
    nz = rows_n // (NX * NC)
    chips = NX * ny
    list_len = select.shape[0]
    slots = list_len // ny
    depth, col_w = w_img.shape
    emb_w = col_w * ny
    out_rows = depth // rows_n
    half = nz // 2
    vmem, smem = pltpu.VMEM, pltpu.SMEM
    dma = pltpu.SemaphoreType.DMA
    out = jax.ShapeDtypeStruct((out_rows, col_w), f32)
    scratch = [
        vmem((2, list_len, depth), bf16),
        vmem((2, list_len, col_w), f32),
        vmem((ny, 2, slots, col_w), f32),
        vmem((2, slots, 1), f32),
        vmem((nz, slots, emb_w), bf16),
        vmem((chips, NC, slots, emb_w), bf16),
        vmem((nz, slots, emb_w), f32),
        vmem((chips, NC, slots, emb_w), f32),
        vmem((half, slots, emb_w), f32),
        vmem((max(nz - half - 1, 1), slots, emb_w), f32),
        vmem((chips, slots, emb_w), f32),
        vmem((chips, slots, emb_w), f32),
        vmem((chips, slots, emb_w), f32),
        vmem((ny, 2, slots, col_w), bf16),
        vmem((ny, 2, slots, col_w), bf16),
        vmem((2, nz, NX, NC, out_rows, col_w), f32),
        vmem((2, nz, NX, out_rows, col_w), f32),
        vmem((2, nz, NX, out_rows, col_w), f32),
        vmem((NX - 1, 2, nz, out_rows, col_w), f32),
        vmem((2, nz, out_rows, col_w), f32),
        vmem((nz - 1, 2, out_rows, col_w), f32),
        dma((ny - 1, 2)),
        dma((half, ZCH, 2)),
        dma((max(nz - half - 1, 1), ZCH, 2)),
        dma((chips - 1, 2)),
        dma((chips, 2)),
        dma((half, ZCH, 2)),
        dma((max(nz - half - 1, 1), ZCH, 2)),
        dma((chips // TILE, 2)),
        dma((chips - 1, 2)),
        dma((ny - 1, 2)),
        dma((2,)),
        dma((NX - 1, 2)),
        dma((nz - 1, 2)),
    ]
    whole = pl.BlockSpec(memory_space=vmem)
    scalar = pl.BlockSpec(memory_space=smem)
    return pl.pallas_call(
        functools.partial(kernel, (nz, ny, chips)),
        out_shape=(out, out),
        in_specs=[whole] * 5 + [scalar] * 4,
        out_specs=(whole, whole),
        scratch_shapes=scratch,
        compiler_params=pltpu.CompilerParams(
            collective_id=0, has_side_effects=True, vmem_limit_bytes=60 << 20
        ),
        name="learner_step",
    )(
        pool_img, pool_txt, w_img, w_txt, select[:, None], counts,
        logit_scale, logit_bias, loss_scale,
    )


def solution(mesh):
    in_specs = (
        P("rows", None),
        P("rows", None),
        P(None, "tower"),
        P(None, "tower"),
        P(),
        P(),
        P(),
        P("rows"),
        P("rows"),
    )
    out_specs = (P("rows", "tower"), P("rows", "tower"))
    return jax.shard_map(
        on_device, mesh=mesh, in_specs=in_specs, out_specs=out_specs, check_vma=False
    )
```

time: 1020 us -> 125 us (0.12)
  waiting for transfers between devices: 637 us -> 0 us
  blocking collectives: 121 us -> 0 us
  Pallas kernels: 0 us -> 118 us
  local copies, waits for them, and re-layouts: 89 us -> 3.33 us
  loops' own time: 82.7 us -> 0 us
  starting transfers between devices: 38.4 us -> 0 us
  matrix products: 19.1 us -> 0 us
  between operations: 17.3 us -> 3.24 us
    unnamed x6 -> x0, waiting for transfers between devices: 326 us -> none
    all_gather x2 -> x0, waiting for transfers between devices: 235 us -> none  [the longest x1 135 us: on_device(): lax.all_gather(part_img, 'rows', axis=0, tiled=True)]
    pallas_call x0 -> x1, Pallas kernels: none -> 118 us  [on_device(): pl.pallas_call(functools.partial(kernel, (nz, ny, chips)), out_shape=(out...]
    another operation x1 -> x0, loops' own time: 82.7 us -> none  [entering(): return lax.fori_loop(0, size, lap, start)]
    dynamic_slice x130 -> x0, local copies, waits for them, and re-layouts: 77.4 us -> none  [the longest x128 76.2 us: lap(): new = combine(before, everything[k])]
    all_to_all x2 -> x0, blocking collectives: 57.8 us -> none  [the longest x1 35 us: on_device(): lax.all_to_all(back_txt, 'rows', split_axis=0, concat_axis=0, tiled=True)]
    reduce_scatter x2 -> x0, waiting for transfers between devices: 47.5 us -> none  [the longest x1 29.4 us: on_device(): lax.psum_scatter(side_txt, 'tower', scatter_dimension=1, tiled=True)]
    all_to_all x3 -> x0, starting transfers between devices: 38 us -> none  [the longest x1 17.8 us: on_device(): lax.all_to_all(sent_txt, 'rows', split_axis=0, concat_axis=0, tiled=True)]
  transfers between devices with their start and end apart: 8 -> 0, of which waited for: 7 -> 0; matrix products, arithmetic and copies ran while one was open for 2% -> 0% of each run, Pallas kernels for 0% -> 0%
where the time goes in v1:
time: 125 us
  Pallas kernels  118 us (94%)
  local copies, waits for them, and re-layouts  3.33 us (3%)
  between operations  3.24 us (3%)
    pallas_call x1, Pallas kernels, on_device(): pl.pallas_call(functools.partial(kernel, (nz, ny, chips)), out_shape=(out...  118 us
    unnamed x6, local copies, waits for them, and re-layouts  2.54 us

profile of v1, /device:TPU:1, one launch (start us, length us, event | category | flops | bytes accessed | tf_op | source)
XLA Modules:
  0.0 124.9 jit_solution(8540302540847210297)
XLA Ops:
  3.2 0.0 copy-start.1
  3.2 0.7 copy-done.1
  3.9 0.8 copy.11.sel
  4.7 118.3 %learner_step.1 = (f32[8,128]{1,0:T(8,128)}, f32[8,128]{1,0:T(8,128)}) custom-call(bf16[512,1024]{1,0:T(8,128)(2,1)} %pool_img.1, bf16[512,1024]{1,0:T(8,128)(2,1)} %pool_txt.1, bf16[1024,128]{1,0:T(8,128)(2,1)} %w_img.1, bf16[1024,128]{1,0:T(8,128)(2,1)} %w_txt.1, s32[256,1]{1,0:T(8,128)} %copy.11.sel, s32[1]{0:T(128)S(6)} %copy.17.cnt, f32[1]{0:T(128)S(6)} %copy.14.temper, ...), custom_call_target="tpu_custom_call" | custom-call | tf_op jit(solution)/shard_map/learner_step/pallas_call | solution.py:353
  123.0 0.0 copy-start
  123.0 1.3 %copy.18 = f32[8,128]{1,0:T(8,128)} copy(f32[8,128]{1,0:T(8,128)} %get-tuple-element.4) | data formatting | bytes 8192
  124.3 0.0 copy-done
  124.3 0.6 copy.19
Async XLA Ops:
  3.2 0.7 copy-start.1
  123.0 1.3 %copy-start = (f32[8,128]{1,0:T(8,128)S(1)}, f32[8,128]{1,0:T(8,128)}, u32[]{:S(2)}) copy-start(f32[8,128]{1,0:T(8,128)} %get-tuple-element.5) | copy-start | bytes 12292

commit v2 on v1

v2 whole, which is shorter than its diff:
```python
import functools

import jax
import jax.numpy as jnp
from jax import lax
from jax.experimental import pallas as pl
from jax.experimental.pallas import tpu as pltpu
from jax.sharding import PartitionSpec as P

bf16 = jnp.bfloat16
f32 = jnp.float32
eps = 1e-06

NX, NC = 4, 2
LRN = 128
GROUP, TILE = 4, 4
ZCH = 2
NEAR_Z = 2


def dot(a, b, ca=1, cb=0):
    return lax.dot_general(a, b, (((ca,), (cb,)), ((), ())), preferred_element_type=f32)


def chip_order(nx, ny):
    ring = lambda d, n: min(d, n - d)
    places = [(dx, dy) for dx in range(nx) for dy in range(ny)]
    return sorted(places, key=lambda p: (ring(p[0], nx) + ring(p[1], ny), p))


def kernel(
    cfg,
    h_pool_img, h_pool_txt, h_w_img, h_w_txt, h_sel, h_cnt, h_temper, h_bias, h_loss_scale,
    out_img, out_txt,
    pool, w, sel, cnt, temper, bias, loss_scale,
    feats, feats_t, proj, unit, norm, zbuf, pbuf, gimg, gtxt, rs_out, rs_up, rs_dn,
    rcore, sbuf, rxy, gp, gpr, gw, gwc, gx, gxr, gz, gzr,
    in_sem, y_sem, za_up, za_dn, xy_sem, cf_sem, zr_up, zr_dn, cr_sem, xr_sem, yb_sem,
    fc_sem, fx_sem, fz_sem,
):
    nz, ny = cfg
    row, y = lax.axis_index("rows"), lax.axis_index("tower")
    c = row % NC
    x = row // NC % NX
    z = row // (NC * NX)
    most_up, most_dn = nz // 2, nz - nz // 2 - 1
    order = chip_order(NX, ny)
    groups, tiles = nz // GROUP, len(order) // TILE
    slots = unit.shape[1]
    emb_w = zbuf.shape[2]
    col_w = proj.shape[2]
    sends = []

    def at(dz=0, dx=0, dy=0, dc=0):
        r = ((z + dz + nz) % nz * NX + (x + dx + NX) % NX) * NC + (c + dc) % NC
        return (r, (y + dy + ny) % ny)

    def send(src, dst, sems, where):
        copy = pltpu.make_async_remote_copy(
            src_ref=src, dst_ref=dst, send_sem=sems.at[0], recv_sem=sems.at[1],
            device_id=where, device_id_type=pl.DeviceIdType.MESH,
        )
        copy.start()
        sends.append(copy)

    def arrived(ref, sems):
        pltpu.make_async_remote_copy(
            src_ref=ref, dst_ref=ref, send_sem=sems.at[0], recv_sem=sems.at[1],
            device_id=at(), device_id_type=pl.DeviceIdType.MESH,
        ).wait_recv()

    loads = [
        pltpu.make_async_copy(src, dst, in_sem.at[n])
        for n, (src, dst) in enumerate((
            (h_sel, sel), (h_pool_img, pool.at[0]), (h_w_img, w.at[0]),
            (h_pool_txt, pool.at[1]), (h_w_txt, w.at[1]), (h_cnt, cnt),
            (h_temper, temper), (h_bias, bias), (h_loss_scale, loss_scale),
        ))
    ]
    for load in loads:
        load.start()
    partners = [at(dx=dx, dy=dy) for dx, dy in order[1:]]
    partners += [at(dz=dz) for dz in [d for d in range(1, nz) if min(d, nz - d) <= NEAR_Z]] + [at(dc=1)]
    barrier = pltpu.get_barrier_semaphore()
    for there in partners:
        pl.semaphore_signal(
            barrier, inc=1, device_id=there, device_id_type=pl.DeviceIdType.MESH
        )

    loads[0].wait()
    rows_at = lax.broadcasted_iota(jnp.int32, (pool.shape[1], sel.shape[0]), 0)
    pick = jnp.where(sel[...][None, :] == rows_at, 1.0, 0.0).astype(bf16)

    def project(side):
        loads[1 + 2 * side].wait()
        feats[side] = dot(pick, pool[side], 0, 0).astype(bf16)
        loads[2 + 2 * side].wait()
        proj[side] = dot(feats[side], w[side])

    def deal(side):
        for dy in (2, 1, 3):
            if dy >= ny:
                continue
            yy = (y + dy) % ny
            send(
                proj.at[side, pl.ds(pl.multiple_of(yy * slots, slots), slots)],
                unit.at[side * ny + y], y_sem.at[side, dy - 1], at(dy=dy),
            )
        unit[side * ny + y] = proj[side, pl.ds(pl.multiple_of(y * slots, slots), slots)]

    def embed(side):
        for dy in range(1, ny):
            arrived(unit.at[side * ny + (y - dy + ny) % ny], y_sem.at[side, dy - 1])
        parts = [unit[side * ny + k] for k in range(ny)]
        square = sum(jnp.sum(part * part, axis=1, keepdims=True) for part in parts)
        norm[side] = lax.rsqrt(square + eps)
        for k in range(ny):
            rows = parts[k] * norm[side]
            unit[side * ny + k] = rows
            emb = jnp.where(live, rows, 0.0).astype(bf16)
            if side == 0:
                zbuf[0, :, k * col_w:(k + 1) * col_w] = emb
            else:
                pbuf[0, 0, :, k * col_w:(k + 1) * col_w] = emb

    def spot(offset):
        return 2 * offset if offset >= 0 else -2 * offset - 1

    zrows = slots // ZCH

    def ring_send(p):
        k = 2 * p - 2
        for h in range(ZCH):
            rows = pl.ds(h * zrows, zrows)
            for sign, most, sems in ((1, most_up, za_up), (-1, most_dn, za_dn)):
                if k > most:
                    continue
                have = zbuf.at[spot(-sign * k), rows]
                if k:
                    arrived(have, sems.at[k - 1, h])
                for step in (2, 1):
                    if k + step <= most:
                        send(have, zbuf.at[spot(-sign * (k + step)), rows],
                             sems.at[k + step - 1, h], at(dz=sign * step))

    def ring_odd(p):
        k = 2 * p - 1
        for h in range(ZCH):
            rows = pl.ds(h * zrows, zrows)
            for sign, most, sems in ((1, most_up, za_up), (-1, most_dn, za_dn)):
                if k <= most:
                    arrived(zbuf.at[spot(-sign * k), rows], sems.at[k - 1, h])

    def spread():
        for n, (dx, dy) in enumerate(order[1:]):
            send(pbuf.at[0, 0], pbuf.at[n + 1, 0], xy_sem.at[n], at(dx=dx, dy=dy))
        send(pbuf.at[0, 0], pbuf.at[0, 1], cf_sem.at[0], at(dc=1))

    def hand_over(t):
        for n in range(t * TILE, (t + 1) * TILE):
            if n:
                arrived(pbuf.at[n, 0], xy_sem.at[n - 1])
                send(pbuf.at[n, 0], pbuf.at[n, 1], cf_sem.at[n], at(dc=1))

    def tile_ready(t):
        for n in range(t * TILE, (t + 1) * TILE):
            arrived(pbuf.at[n, 1], cf_sem.at[n])

    def pair_tile(g, t):
        img = zbuf[g * GROUP:(g + 1) * GROUP].reshape(GROUP * slots, emb_w)
        txt = pbuf[t * TILE:(t + 1) * TILE].reshape(TILE * NC * slots, emb_w)
        logits = temper[0] * dot(img, txt, 1, 1) + bias[0]
        weights = 1.0 / (1.0 + jnp.exp(-logits))
        if g == 0 and t == 0:
            i = lax.broadcasted_iota(jnp.int32, logits.shape, 0)
            j = lax.broadcasted_iota(jnp.int32, logits.shape, 1)
            weights = jnp.where((i == j) & (i < slots), 0.0, weights)
        weights = weights.astype(bf16)
        to_img = dot(weights, txt).reshape(GROUP, slots, emb_w)
        to_txt = dot(weights, img, 0, 0).reshape(TILE, NC, slots, emb_w)
        at_img = slice(g * GROUP, (g + 1) * GROUP)
        at_txt = slice(t * TILE, (t + 1) * TILE)
        gimg[at_img] = gimg[at_img] + to_img if g in begun_img else to_img
        gtxt[at_txt] = gtxt[at_txt] + to_txt if t in begun_txt else to_txt
        begun_img.add(g)
        begun_txt.add(t)

    begun_img, begun_txt = set(), set()

    def ring_sum(p):
        k = most_up + 2 - 2 * p
        for h in range(ZCH):
            rows = pl.ds(h * zrows, zrows)
            total = None
            for sign, most, got, sems in (
                (1, most_up, rs_up, zr_up), (-1, most_dn, rs_dn, zr_dn)
            ):
                if k <= most:
                    here = spot(sign * k) if k < most_up else spot(-most_up)
                    if total is None or k:
                        total = gimg[here, rows]
                    for far in (k + 1, k + 2):
                        if far <= most:
                            arrived(got.at[far - 1, rows], sems.at[far - 1, h])
                            total = total + got[far - 1, rows].astype(f32)
                    if k:
                        rs_out[here, rows] = total.astype(bf16)
                        send(rs_out.at[here, rows], got.at[k - 1, rows],
                             sems.at[k - 1, h], at(dz=2 * sign))
                if 1 <= k - 1 <= most:
                    here = spot(sign * (k - 1))
                    rs_out[here, rows] = gimg[here, rows].astype(bf16)
                    send(rs_out.at[here, rows], got.at[k - 2, rows],
                         sems.at[k - 2, h], at(dz=sign))
            if k == 0:
                gimg[0, rows] = total

    def core_send(t):
        part = pl.ds(t * TILE, TILE)
        send(gtxt.at[part, 1], rcore.at[part], cr_sem.at[t], at(dc=1))

    def plane_send(t):
        part = pl.ds(t * TILE, TILE)
        arrived(rcore.at[part], cr_sem.at[t])
        for n in range(t * TILE, (t + 1) * TILE):
            both = gtxt[n, 0] + rcore[n]
            if n == 0:
                gtxt[0, 0] = both
            else:
                sbuf[n] = both.astype(sbuf.dtype)
                dx, dy = order[n]
                send(sbuf.at[n], rxy.at[n], xr_sem.at[n - 1], at(dx=-dx, dy=-dy))

    def finish(side, total, emb, other):
        own = temper[0] * jnp.sum(emb * other, axis=1, keepdims=True) + bias[0]
        own = (-1.0 / (1.0 + jnp.exp(own))).astype(bf16).astype(f32)
        factor = loss_scale[0] * temper[0] / (LRN * nz * NX * NC)
        grad = jnp.where(live, factor * (total + own * other), 0.0)
        inner = sum(
            jnp.sum(unit[side * ny + k] * grad[:, k * col_w:(k + 1) * col_w],
                    axis=1, keepdims=True)
            for k in range(ny)
        )
        for k in range(ny):
            part = grad[:, k * col_w:(k + 1) * col_w]
            gp[side * ny + k] = (
                norm[side] * (part - unit[side * ny + k] * inner)
            ).astype(bf16)
        for dy in (2, 1, 3):
            if dy < ny:
                send(gp.at[side * ny + (y + dy) % ny], gpr.at[side * ny + y],
                     yb_sem.at[side, dy - 1], at(dy=dy))
        gpr[side * ny + y] = gp[side * ny + y]

    def weight_grad(side):
        for dy in range(1, ny):
            arrived(gpr.at[side * ny + (y - dy + ny) % ny], yb_sem.at[side, dy - 1])
        grad = gpr[side * ny:(side + 1) * ny].reshape(ny * slots, col_w)
        gw[side] = dot(feats_t[side], grad).reshape(gw.shape[1:])
        send(gw.at[side, :, :, 1 - c], gwc.at[side], fc_sem.at[side], at(dc=1))

    def over_x(side):
        arrived(gwc.at[side], fc_sem.at[side])
        gx[side] = gw[side, :, :, c] + gwc[side]
        for dx in (2, 1, 3):
            if dx < NX:
                send(gx.at[side, :, (x + dx) % NX], gxr.at[side, dx - 1],
                     fx_sem.at[side, dx - 1], at(dx=dx))

    def over_z(side):
        total = gx[side, :, x]
        for dx in range(1, NX):
            arrived(gxr.at[side, dx - 1], fx_sem.at[side, dx - 1])
            total = total + gxr[side, dx - 1]
        gz[side] = total
        for dz in sorted(range(1, nz), key=lambda d: -min(d, nz - d)):
            send(gz.at[side, (z + dz) % nz], gzr.at[side, dz - 1],
                 fz_sem.at[side, dz - 1], at(dz=dz))

    def collect(side, out):
        total = gz[side, z]
        for dz in range(1, nz):
            arrived(gzr.at[side, dz - 1], fz_sem.at[side, dz - 1])
            total = total + gzr[side, dz - 1]
        out[...] = total

    project(0)
    for load in loads[5:]:
        load.wait()
    slot_at = y * slots + lax.broadcasted_iota(jnp.int32, (slots, 1), 0)
    live = slot_at < cnt[0]
    pl.semaphore_wait(barrier, len(partners))
    deal(0)
    project(1)
    deal(1)
    embed(0)
    ring_send(1)
    embed(1)
    spread()
    for side in range(2):
        feats_t[side] = feats[side].T

    phases = [
        [(k, t) for t in range(k)] + [(g, k) for g in range(k + 1)] for k in range(groups - 1)
    ]
    phases.append([(groups - 1, t) for t in range(tiles)])
    opened = 0
    for p in range(1, most_up // 2 + 2):
        if p > 1:
            ring_send(p)
            ring_odd(p - 1)
        queue = []
        while opened < groups and p > 1 and (
            (opened + 1) * GROUP - 1 <= min(4 * (p - 1), nz - 1)
        ):
            if opened >= p - 1 and opened:
                hand_over(opened)
            tile_ready(opened)
            queue += phases[opened]
            opened += 1
        if p <= most_up // 2:
            for tile in queue:
                pair_tile(*tile)
            if p <= tiles:
                hand_over(p - 1)
    early = [tile for tile in queue if tile[0] < groups - 1]
    for tile in early:
        pair_tile(*tile)
    for t in range(tiles):
        pair_tile(groups - 1, t)
        if t < tiles - 1:
            core_send(t)
    ring_sum(1)
    for g in range(groups - 2, -1, -1):
        pair_tile(g, tiles - 1)
    core_send(tiles - 1)
    done = 0
    for p in range(2, most_up // 2 + 1):
        for t in range(done, min(done + 2, tiles)):
            plane_send(t)
        done = min(done + 2, tiles)
        ring_sum(p)
    for t in range(done, tiles):
        plane_send(t)
    emb_i = zbuf[0].astype(f32)
    emb_t = pbuf[0, 0].astype(f32)
    for n in range(1, len(order)):
        arrived(rxy.at[n], xr_sem.at[n - 1])
    total = gtxt[0, 0]
    for n in range(1, len(order)):
        total = total + rxy[n].astype(f32)
    finish(1, total, emb_t, emb_i)
    ring_sum(most_up // 2 + 1)
    finish(0, gimg[0], emb_i, emb_t)
    weight_grad(1)
    weight_grad(0)
    over_x(1)
    over_x(0)
    over_z(1)
    over_z(0)
    collect(1, out_txt)
    collect(0, out_img)
    for copy in sends:
        copy.wait_send()


def on_device(
    pool_img, pool_txt, w_img, w_txt, logit_scale, logit_bias, loss_scale, select, counts
):
    ny = lax.axis_size("tower")
    rows_n = lax.axis_size("rows")
    nz = rows_n // (NX * NC)
    chips = NX * ny
    list_len = select.shape[0]
    slots = list_len // ny
    depth, col_w = w_img.shape
    emb_w = col_w * ny
    out_rows = depth // rows_n
    most_up, most_dn = nz // 2, nz - nz // 2 - 1
    vmem, smem = pltpu.VMEM, pltpu.SMEM
    dma = pltpu.SemaphoreType.DMA
    out = jax.ShapeDtypeStruct((out_rows, col_w), f32)
    scratch = [
        vmem((2,) + pool_img.shape, bf16),
        vmem((2, depth, col_w), bf16),
        vmem((list_len,), jnp.int32),
        smem((1,), jnp.int32),
        smem((1,), f32),
        smem((1,), f32),
        smem((1,), f32),
        vmem((2, list_len, depth), bf16),
        vmem((2, depth, list_len), bf16),
        vmem((2, list_len, col_w), f32),
        vmem((2 * ny, slots, col_w), f32),
        vmem((2, slots, 1), f32),
        vmem((nz, slots, emb_w), bf16),
        vmem((chips, NC, slots, emb_w), bf16),
        vmem((nz, slots, emb_w), f32),
        vmem((chips, NC, slots, emb_w), f32),
        vmem((nz, slots, emb_w), bf16),
        vmem((most_up, slots, emb_w), bf16),
        vmem((most_dn, slots, emb_w), bf16),
        vmem((chips, slots, emb_w), f32),
        vmem((chips, slots, emb_w), bf16),
        vmem((chips, slots, emb_w), bf16),
        vmem((2 * ny, slots, col_w), bf16),
        vmem((2 * ny, slots, col_w), bf16),
        vmem((2, nz, NX, NC, out_rows, col_w), f32),
        vmem((2, nz, NX, out_rows, col_w), f32),
        vmem((2, nz, NX, out_rows, col_w), f32),
        vmem((2, NX - 1, nz, out_rows, col_w), f32),
        vmem((2, nz, out_rows, col_w), f32),
        vmem((2, nz - 1, out_rows, col_w), f32),
        dma((9,)),
        dma((2, ny - 1, 2)),
        dma((most_up, ZCH, 2)),
        dma((most_dn, ZCH, 2)),
        dma((chips - 1, 2)),
        dma((chips, 2)),
        dma((most_up, ZCH, 2)),
        dma((most_dn, ZCH, 2)),
        dma((chips // TILE, 2)),
        dma((chips - 1, 2)),
        dma((2, ny - 1, 2)),
        dma((2, 2)),
        dma((2, NX - 1, 2)),
        dma((2, nz - 1, 2)),
    ]
    whole = pl.BlockSpec(memory_space=vmem)
    placed = pl.BlockSpec(memory_space=pl.ANY)
    return pl.pallas_call(
        functools.partial(kernel, (nz, ny)),
        out_shape=(out, out),
        in_specs=[placed] * 4 + [pl.BlockSpec(memory_space=pltpu.HBM)] * 5,
        out_specs=(whole, whole),
        scratch_shapes=scratch,
        compiler_params=pltpu.CompilerParams(
            collective_id=0, has_side_effects=True, vmem_limit_bytes=60 << 20
        ),
        name="learner_step",
    )(
        pool_img, pool_txt, w_img, w_txt, select, counts,
        logit_scale, logit_bias, loss_scale,
    )


def solution(mesh):
    in_specs = (
        P("rows", None),
        P("rows", None),
        P(None, "tower"),
        P(None, "tower"),
        P(),
        P(),
        P(),
        P("rows"),
        P("rows"),
    )
    out_specs = (P("rows", "tower"), P("rows", "tower"))
    return jax.shard_map(
        on_device, mesh=mesh, in_specs=in_specs, out_specs=out_specs, check_vma=False
    )
```

time: 125 us -> 96.7 us (0.77)
  Pallas kernels: 118 us -> 91.4 us
  local copies, waits for them, and re-layouts: 3.33 us -> 1.86 us
    pallas_call x1, Pallas kernels: 118 us -> 91.4 us  [on_device(): pl.pallas_call(functools.partial(kernel, (nz, ny)), out_shape=(out, out),...]
    unnamed x6 -> x4, local copies, waits for them, and re-layouts: 2.54 us -> 1.86 us
where the time goes in v2:
time: 96.7 us; the launch traced here: 96.5 us
  Pallas kernels  91.4 us (95%)
  between operations  3.23 us (3%)
  local copies, waits for them, and re-layouts  1.86 us (2%)
    pallas_call x1, Pallas kernels, on_device(): pl.pallas_call(functools.partial(kernel, (nz, ny)), out_shape=(out, out),...  91.4 us

profile of v2, /device:TPU:1, one launch (start us, length us, event | category | flops | bytes accessed | tf_op | source)
XLA Modules:
  0.0 96.5 jit_solution(11646302608425460533)
XLA Ops:
  3.2 91.4 %learner_step.1 = (f32[8,128]{1,0:T(8,128)}, f32[8,128]{1,0:T(8,128)}) custom-call(bf16[512,1024]{1,0:T(8,128)(2,1)} %h_pool_img.1, bf16[512,1024]{1,0:T(8,128)(2,1)} %h_pool_txt.1, bf16[1024,128]{1,0:T(8,128)(2,1)} %h_w_img.1, bf16[1024,128]{1,0:T(8,128)(2,1)} %h_w_txt.1, s32[256]{0:T(256)} %h_sel.1, s32[1]{0:T(128)S(6)} %copy.16.h_cnt, ...), custom_call_target="tpu_custom_call" | custom-call | tf_op jit(solution)/shard_map/learner_step/pallas_call | solution.py:431
  94.6 0.0 copy-start
  94.6 1.3 %copy.17 = f32[8,128]{1,0:T(8,128)} copy(f32[8,128]{1,0:T(8,128)} %get-tuple-element.4) | data formatting | bytes 8192
  95.9 0.0 copy-done
  95.9 0.6 copy.18
Async XLA Ops:
  94.6 1.3 %copy-start = (f32[8,128]{1,0:T(8,128)S(1)}, f32[8,128]{1,0:T(8,128)}, u32[]{:S(2)}) copy-start(f32[8,128]{1,0:T(8,128)} %get-tuple-element.5) | copy-start | bytes 12292

commit v3 on v2

--- a/solution.py
+++ b/solution.py
@@ -13,7 +13,15 @@
 
 NX, NC = 4, 2
 LRN = 128
-GROUP, TILE = 4, 4
+PLAN = {
+    2: [("hand", 0)],
+    3: [("hand", 1), ("ready", 0), ("pair", 0, 0), ("pair", 1, 0),
+        ("ready", 1), ("pair", 0, 1), ("pair", 1, 1), ("hand", 2)],
+    4: [("hand", 3), ("pair", 2, 0), ("pair", 2, 1),
+        ("ready", 2), ("pair", 0, 2), ("pair", 1, 2), ("pair", 2, 2)],
+    5: [("ready", 3)],
+}
+GROUPS, TILE = (0, 5, 9, 13, 16), 4
 ZCH = 2
 NEAR_Z = 2
 
@@ -30,9 +38,9 @@
 
 def kernel(
     cfg,
-    h_pool_img, h_pool_txt, h_w_img, h_w_txt, h_sel, h_cnt, h_temper, h_bias, h_loss_scale,
+    h_pool_img, h_pool_txt, h_w_img, h_w_txt, h_sel, cnt, temper, bias, loss_scale,
     out_img, out_txt,
-    pool, w, sel, cnt, temper, bias, loss_scale,
+    pool, w, sel,
     feats, feats_t, proj, unit, norm, zbuf, pbuf, gimg, gtxt, rs_out, rs_up, rs_dn,
     rcore, sbuf, rxy, gp, gpr, gw, gwc, gx, gxr, gz, gzr,
     in_sem, y_sem, za_up, za_dn, xy_sem, cf_sem, zr_up, zr_dn, cr_sem, xr_sem, yb_sem,
@@ -43,9 +51,9 @@
     c = row % NC
     x = row // NC % NX
     z = row // (NC * NX)
-    most_up, most_dn = nz // 2, nz - nz // 2 - 1
+    most_up = nz // 2
     order = chip_order(NX, ny)
-    groups, tiles = nz // GROUP, len(order) // TILE
+    groups, tiles = len(GROUPS) - 1, len(order) // TILE
     slots = unit.shape[1]
     emb_w = zbuf.shape[2]
     col_w = proj.shape[2]
@@ -73,8 +81,7 @@
         pltpu.make_async_copy(src, dst, in_sem.at[n])
         for n, (src, dst) in enumerate((
             (h_sel, sel), (h_pool_img, pool.at[0]), (h_w_img, w.at[0]),
-            (h_pool_txt, pool.at[1]), (h_w_txt, w.at[1]), (h_cnt, cnt),
-            (h_temper, temper), (h_bias, bias), (h_loss_scale, loss_scale),
+            (h_pool_txt, pool.at[1]), (h_w_txt, w.at[1]),
         ))
     ]
     for load in loads:
@@ -124,15 +131,21 @@
                 pbuf[0, 0, :, k * col_w:(k + 1) * col_w] = emb
 
     def spot(offset):
-        return 2 * offset if offset >= 0 else -2 * offset - 1
+        return 2 * offset if 0 <= offset < most_up else 2 * abs(offset) - 1
 
     zrows = slots // ZCH
+
+    def ways(h, *args):
+        up = h < ZCH // 2
+        return [
+            (1, most_up - (not up), *args[0::2]), (-1, most_up - up, *args[1::2])
+        ]
 
     def ring_send(p):
         k = 2 * p - 2
         for h in range(ZCH):
             rows = pl.ds(h * zrows, zrows)
-            for sign, most, sems in ((1, most_up, za_up), (-1, most_dn, za_dn)):
+            for sign, most, sems in ways(h, za_up, za_dn):
                 if k > most:
                     continue
                 have = zbuf.at[spot(-sign * k), rows]
@@ -147,7 +160,7 @@
         k = 2 * p - 1
         for h in range(ZCH):
             rows = pl.ds(h * zrows, zrows)
-            for sign, most, sems in ((1, most_up, za_up), (-1, most_dn, za_dn)):
+            for sign, most, sems in ways(h, za_up, za_dn):
                 if k <= most:
                     arrived(zbuf.at[spot(-sign * k), rows], sems.at[k - 1, h])
 
@@ -167,18 +180,19 @@
             arrived(pbuf.at[n, 1], cf_sem.at[n])
 
     def pair_tile(g, t):
-        img = zbuf[g * GROUP:(g + 1) * GROUP].reshape(GROUP * slots, emb_w)
+        at_img = slice(GROUPS[g], GROUPS[g + 1])
+        count = GROUPS[g + 1] - GROUPS[g]
+        img = zbuf[at_img].reshape(count * slots, emb_w)
         txt = pbuf[t * TILE:(t + 1) * TILE].reshape(TILE * NC * slots, emb_w)
-        logits = temper[0] * dot(img, txt, 1, 1) + bias[0]
+        logits = temper_val * dot(img, txt, 1, 1) + bias_val
         weights = 1.0 / (1.0 + jnp.exp(-logits))
         if g == 0 and t == 0:
             i = lax.broadcasted_iota(jnp.int32, logits.shape, 0)
             j = lax.broadcasted_iota(jnp.int32, logits.shape, 1)
             weights = jnp.where((i == j) & (i < slots), 0.0, weights)
         weights = weights.astype(bf16)
-        to_img = dot(weights, txt).reshape(GROUP, slots, emb_w)
+        to_img = dot(weights, txt).reshape(count, slots, emb_w)
         to_txt = dot(weights, img, 0, 0).reshape(TILE, NC, slots, emb_w)
-        at_img = slice(g * GROUP, (g + 1) * GROUP)
         at_txt = slice(t * TILE, (t + 1) * TILE)
         gimg[at_img] = gimg[at_img] + to_img if g in begun_img else to_img
         gtxt[at_txt] = gtxt[at_txt] + to_txt if t in begun_txt else to_txt
@@ -192,11 +206,9 @@
         for h in range(ZCH):
             rows = pl.ds(h * zrows, zrows)
             total = None
-            for sign, most, got, sems in (
-                (1, most_up, rs_up, zr_up), (-1, most_dn, rs_dn, zr_dn)
-            ):
+            for sign, most, got, sems in ways(h, rs_up, rs_dn, zr_up, zr_dn):
                 if k <= most:
-                    here = spot(sign * k) if k < most_up else spot(-most_up)
+                    here = spot(sign * k)
                     if total is None or k:
                         total = gimg[here, rows]
                     for far in (k + 1, k + 2):
@@ -232,9 +244,8 @@
                 send(sbuf.at[n], rxy.at[n], xr_sem.at[n - 1], at(dx=-dx, dy=-dy))
 
     def finish(side, total, emb, other):
-        own = temper[0] * jnp.sum(emb * other, axis=1, keepdims=True) + bias[0]
+        own = temper_val * jnp.sum(emb * other, axis=1, keepdims=True) + bias_val
         own = (-1.0 / (1.0 + jnp.exp(own))).astype(bf16).astype(f32)
-        factor = loss_scale[0] * temper[0] / (LRN * nz * NX * NC)
         grad = jnp.where(live, factor * (total + own * other), 0.0)
         inner = sum(
             jnp.sum(unit[side * ny + k] * grad[:, k * col_w:(k + 1) * col_w],
@@ -285,8 +296,8 @@
         out[...] = total
 
     project(0)
-    for load in loads[5:]:
-        load.wait()
+    temper_val, bias_val = temper[0], bias[0]
+    factor = loss_scale[0] * temper_val / (LRN * nz * NX * NC)
     slot_at = y * slots + lax.broadcasted_iota(jnp.int32, (slots, 1), 0)
     live = slot_at < cnt[0]
     pl.semaphore_wait(barrier, len(partners))
@@ -300,32 +311,11 @@
     for side in range(2):
         feats_t[side] = feats[side].T
 
-    phases = [
-        [(k, t) for t in range(k)] + [(g, k) for g in range(k + 1)] for k in range(groups - 1)
-    ]
-    phases.append([(groups - 1, t) for t in range(tiles)])
-    opened = 0
-    for p in range(1, most_up // 2 + 2):
-        if p > 1:
-            ring_send(p)
-            ring_odd(p - 1)
-        queue = []
-        while opened < groups and p > 1 and (
-            (opened + 1) * GROUP - 1 <= min(4 * (p - 1), nz - 1)
-        ):
-            if opened >= p - 1 and opened:
-                hand_over(opened)
-            tile_ready(opened)
-            queue += phases[opened]
-            opened += 1
-        if p <= most_up // 2:
-            for tile in queue:
-                pair_tile(*tile)
-            if p <= tiles:
-                hand_over(p - 1)
-    early = [tile for tile in queue if tile[0] < groups - 1]
-    for tile in early:
-        pair_tile(*tile)
+    for p in range(2, most_up // 2 + 2):
+        ring_send(p)
+        ring_odd(p - 1)
+        for what, *which in PLAN[p]:
+            {"hand": hand_over, "ready": tile_ready, "pair": pair_tile}[what](*which)
     for t in range(tiles):
         pair_tile(groups - 1, t)
         if t < tiles - 1:
@@ -350,11 +340,11 @@
     for n in range(1, len(order)):
         total = total + rxy[n].astype(f32)
     finish(1, total, emb_t, emb_i)
+    weight_grad(1)
     ring_sum(most_up // 2 + 1)
     finish(0, gimg[0], emb_i, emb_t)
-    weight_grad(1)
+    over_x(1)
     weight_grad(0)
-    over_x(1)
     over_x(0)
     over_z(1)
     over_z(0)
@@ -376,18 +366,14 @@
     depth, col_w = w_img.shape
     emb_w = col_w * ny
     out_rows = depth // rows_n
-    most_up, most_dn = nz // 2, nz - nz // 2 - 1
-    vmem, smem = pltpu.VMEM, pltpu.SMEM
+    most_up = nz // 2
+    vmem = pltpu.VMEM
     dma = pltpu.SemaphoreType.DMA
     out = jax.ShapeDtypeStruct((out_rows, col_w), f32)
     scratch = [
         vmem((2,) + pool_img.shape, bf16),
         vmem((2, depth, col_w), bf16),
         vmem((list_len,), jnp.int32),
-        smem((1,), jnp.int32),
-        smem((1,), f32),
-        smem((1,), f32),
-        smem((1,), f32),
         vmem((2, list_len, depth), bf16),
         vmem((2, depth, list_len), bf16),
         vmem((2, list_len, col_w), f32),
@@ -399,7 +385,7 @@
         vmem((chips, NC, slots, emb_w), f32),
         vmem((nz, slots, emb_w), bf16),
         vmem((most_up, slots, emb_w), bf16),
-        vmem((most_dn, slots, emb_w), bf16),
+        vmem((most_up, slots, emb_w), bf16),
         vmem((chips, slots, emb_w), f32),
         vmem((chips, slots, emb_w), bf16),
         vmem((chips, slots, emb_w), bf16),
@@ -411,14 +397,14 @@
         vmem((2, NX - 1, nz, out_rows, col_w), f32),
         vmem((2, nz, out_rows, col_w), f32),
         vmem((2, nz - 1, out_rows, col_w), f32),
-        dma((9,)),
+        dma((5,)),
         dma((2, ny - 1, 2)),
         dma((most_up, ZCH, 2)),
-        dma((most_dn, ZCH, 2)),
+        dma((most_up, ZCH, 2)),
         dma((chips - 1, 2)),
         dma((chips, 2)),
         dma((most_up, ZCH, 2)),
-        dma((most_dn, ZCH, 2)),
+        dma((most_up, ZCH, 2)),
         dma((chips // TILE, 2)),
         dma((chips - 1, 2)),
         dma((2, ny - 1, 2)),
@@ -431,7 +417,7 @@
     return pl.pallas_call(
         functools.partial(kernel, (nz, ny)),
         out_shape=(out, out),
-        in_specs=[placed] * 4 + [pl.BlockSpec(memory_space=pltpu.HBM)] * 5,
+        in_specs=[placed] * 5 + [pl.BlockSpec(memory_space=pltpu.SMEM)] * 4,
         out_specs=(whole, whole),
         scratch_shapes=scratch,
         compiler_params=pltpu.CompilerParams(

time: 96.7 us -> 91.4 us (0.945)
  Pallas kernels: 91.4 us -> 86.1 us
    pallas_call x1, Pallas kernels: 91.4 us -> 86.1 us  [on_device(): pl.pallas_call(functools.partial(kernel, (nz, ny)), out_shape=(out, out),...]
where the time goes in v3:
time: 91.4 us; the launch traced here: 91.1 us
  Pallas kernels  86.1 us (94%)
  between operations  3.23 us (4%)
  local copies, waits for them, and re-layouts  1.86 us (2%)
    pallas_call x1, Pallas kernels, on_device(): pl.pallas_call(functools.partial(kernel, (nz, ny)), out_shape=(out, out),...  86.1 us
    unnamed x4, local copies, waits for them, and re-layouts  1.86 us

profile of v3, /device:TPU:1, one launch (start us, length us, event | category | flops | bytes accessed | tf_op | source)
XLA Modules:
  0.0 91.1 jit_solution(8883575282538780482)
XLA Ops:
  3.2 86.1 %learner_step.1 = (f32[8,128]{1,0:T(8,128)}, f32[8,128]{1,0:T(8,128)}) custom-call(bf16[512,1024]{1,0:T(8,128)(2,1)} %h_pool_img.1, bf16[512,1024]{1,0:T(8,128)(2,1)} %h_pool_txt.1, bf16[1024,128]{1,0:T(8,128)(2,1)} %h_w_img.1, bf16[1024,128]{1,0:T(8,128)(2,1)} %h_w_txt.1, s32[256]{0:T(256)} %h_sel.1, s32[1]{0:T(128)S(6)} %copy.16.cnt, f32[1]{0:T(128)S(6)} %copy.13.temper, ...), custom_call_target="tpu_custom_call" | custom-call | tf_op jit(solution)/shard_map/learner_step/pallas_call | solution.py:417
  89.3 0.0 copy-start
  89.3 1.3 %copy.17 = f32[8,128]{1,0:T(8,128)} copy(f32[8,128]{1,0:T(8,128)} %get-tuple-element.4) | data formatting | bytes 8192
  90.5 0.0 copy-done
  90.6 0.6 copy.18
Async XLA Ops:
  89.3 1.3 %copy-start = (f32[8,128]{1,0:T(8,128)S(1)}, f32[8,128]{1,0:T(8,128)}, u32[]{:S(2)}) copy-start(f32[8,128]{1,0:T(8,128)} %get-tuple-element.5) | copy-start | bytes 12292

commit v4 on v3

--- a/solution.py
+++ b/solution.py
@@ -23,6 +23,7 @@
 }
 GROUPS, TILE = (0, 5, 9, 13, 16), 4
 ZCH = 2
+PARTS = 4
 NEAR_Z = 2
 
 
@@ -41,7 +42,7 @@
     h_pool_img, h_pool_txt, h_w_img, h_w_txt, h_sel, cnt, temper, bias, loss_scale,
     out_img, out_txt,
     pool, w, sel,
-    feats, feats_t, proj, unit, norm, zbuf, pbuf, gimg, gtxt, rs_out, rs_up, rs_dn,
+    feats, feats_t, proj, unit, norm, zbuf, pbuf, gimg, gtxt, wbuf, rs_out, rs_up, rs_dn,
     rcore, sbuf, rxy, gp, gpr, gw, gwc, gx, gxr, gz, gzr,
     in_sem, y_sem, za_up, za_dn, xy_sem, cf_sem, zr_up, zr_dn, cr_sem, xr_sem, yb_sem,
     fc_sem, fx_sem, fz_sem,
@@ -179,11 +180,16 @@
         for n in range(t * TILE, (t + 1) * TILE):
             arrived(pbuf.at[n, 1], cf_sem.at[n])
 
-    def pair_tile(g, t):
+    def pair_tile(g, t, part=None):
         at_img = slice(GROUPS[g], GROUPS[g + 1])
         count = GROUPS[g + 1] - GROUPS[g]
         img = zbuf[at_img].reshape(count * slots, emb_w)
         txt = pbuf[t * TILE:(t + 1) * TILE].reshape(TILE * NC * slots, emb_w)
+        at_txt = slice(t * TILE, (t + 1) * TILE)
+        if part == "txt":
+            to_txt = dot(wbuf[t], img, 0, 0).reshape(TILE, NC, slots, emb_w)
+            gtxt[at_txt] = gtxt[at_txt] + to_txt
+            return
         logits = temper_val * dot(img, txt, 1, 1) + bias_val
         weights = 1.0 / (1.0 + jnp.exp(-logits))
         if g == 0 and t == 0:
@@ -192,11 +198,13 @@
             weights = jnp.where((i == j) & (i < slots), 0.0, weights)
         weights = weights.astype(bf16)
         to_img = dot(weights, txt).reshape(count, slots, emb_w)
+        gimg[at_img] = gimg[at_img] + to_img if g in begun_img else to_img
+        begun_img.add(g)
+        if part == "img":
+            wbuf[t] = weights
+            return
         to_txt = dot(weights, img, 0, 0).reshape(TILE, NC, slots, emb_w)
-        at_txt = slice(t * TILE, (t + 1) * TILE)
-        gimg[at_img] = gimg[at_img] + to_img if g in begun_img else to_img
         gtxt[at_txt] = gtxt[at_txt] + to_txt if t in begun_txt else to_txt
-        begun_img.add(g)
         begun_txt.add(t)
 
     begun_img, begun_txt = set(), set()
@@ -270,29 +278,37 @@
         gw[side] = dot(feats_t[side], grad).reshape(gw.shape[1:])
         send(gw.at[side, :, :, 1 - c], gwc.at[side], fc_sem.at[side], at(dc=1))
 
+    far_first = sorted(range(nz), key=lambda d: -min(d, nz - d))
+    per = nz // PARTS
+
     def over_x(side):
         arrived(gwc.at[side], fc_sem.at[side])
-        gx[side] = gw[side, :, :, c] + gwc[side]
-        for dx in (2, 1, 3):
-            if dx < NX:
-                send(gx.at[side, :, (x + dx) % NX], gxr.at[side, dx - 1],
-                     fx_sem.at[side, dx - 1], at(dx=dx))
+        for part in range(PARTS):
+            piece = pl.ds(part * per, per)
+            for n in range(part * per, (part + 1) * per):
+                there = (z + far_first[n]) % nz
+                gx[side, n] = gw[side, there, :, c] + gwc[side, there]
+            for dx in (2, 1, 3):
+                if dx < NX:
+                    send(gx.at[side, piece, (x + dx) % NX], gxr.at[side, dx - 1, piece],
+                         fx_sem.at[side, dx - 1, part], at(dx=dx))
 
     def over_z(side):
-        total = gx[side, :, x]
-        for dx in range(1, NX):
-            arrived(gxr.at[side, dx - 1], fx_sem.at[side, dx - 1])
-            total = total + gxr[side, dx - 1]
-        gz[side] = total
-        for dz in sorted(range(1, nz), key=lambda d: -min(d, nz - d)):
-            send(gz.at[side, (z + dz) % nz], gzr.at[side, dz - 1],
-                 fz_sem.at[side, dz - 1], at(dz=dz))
+        for part in range(PARTS):
+            piece = pl.ds(part * per, per)
+            total = gx[side, piece, x]
+            for dx in range(1, NX):
+                arrived(gxr.at[side, dx - 1, piece], fx_sem.at[side, dx - 1, part])
+                total = total + gxr[side, dx - 1, piece]
+            gz[side, piece] = total
+            for n in range(part * per, min((part + 1) * per, nz - 1)):
+                send(gz.at[side, n], gzr.at[side, n], fz_sem.at[side, n], at(dz=far_first[n]))
 
     def collect(side, out):
-        total = gz[side, z]
-        for dz in range(1, nz):
-            arrived(gzr.at[side, dz - 1], fz_sem.at[side, dz - 1])
-            total = total + gzr[side, dz - 1]
+        total = gz[side, nz - 1]
+        for n in range(nz - 1):
+            arrived(gzr.at[side, n], fz_sem.at[side, n])
+            total = total + gzr[side, n]
         out[...] = total
 
     project(0)
@@ -317,12 +333,14 @@
         for what, *which in PLAN[p]:
             {"hand": hand_over, "ready": tile_ready, "pair": pair_tile}[what](*which)
     for t in range(tiles):
-        pair_tile(groups - 1, t)
-        if t < tiles - 1:
-            core_send(t)
+        pair_tile(groups - 1, t, "img")
     ring_sum(1)
+    for t in range(tiles - 1):
+        pair_tile(groups - 1, t, "txt")
+        core_send(t)
     for g in range(groups - 2, -1, -1):
         pair_tile(g, tiles - 1)
+    pair_tile(groups - 1, tiles - 1, "txt")
     core_send(tiles - 1)
     done = 0
     for p in range(2, most_up // 2 + 1):
@@ -340,9 +358,9 @@
     for n in range(1, len(order)):
         total = total + rxy[n].astype(f32)
     finish(1, total, emb_t, emb_i)
-    weight_grad(1)
     ring_sum(most_up // 2 + 1)
     finish(0, gimg[0], emb_i, emb_t)
+    weight_grad(1)
     over_x(1)
     weight_grad(0)
     over_x(0)
@@ -383,6 +401,7 @@
         vmem((chips, NC, slots, emb_w), bf16),
         vmem((nz, slots, emb_w), f32),
         vmem((chips, NC, slots, emb_w), f32),
+        vmem((chips // TILE, (GROUPS[-1] - GROUPS[-2]) * slots, TILE * NC * slots), bf16),
         vmem((nz, slots, emb_w), bf16),
         vmem((most_up, slots, emb_w), bf16),
         vmem((most_up, slots, emb_w), bf16),
@@ -409,12 +428,12 @@
         dma((chips - 1, 2)),
         dma((2, ny - 1, 2)),
         dma((2, 2)),
-        dma((2, NX - 1, 2)),
+        dma((2, NX - 1, PARTS, 2)),
         dma((2, nz - 1, 2)),
     ]
     whole = pl.BlockSpec(memory_space=vmem)
     placed = pl.BlockSpec(memory_space=pl.ANY)
-    return pl.pallas_call(
+    step = pl.pallas_call(
         functools.partial(kernel, (nz, ny)),
         out_shape=(out, out),
         in_specs=[placed] * 5 + [pl.BlockSpec(memory_space=pltpu.SMEM)] * 4,
@@ -428,6 +447,15 @@
         pool_img, pool_txt, w_img, w_txt, select, counts,
         logit_scale, logit_bias, loss_scale,
     )
+    return pl.pallas_call(
+        hand_out, out_shape=(out, out), in_specs=[whole] * 2, out_specs=(whole, whole),
+        name="hand_out",
+    )(*step)
+
+
+def hand_out(img, txt, out_img, out_txt):
+    out_img[...] = img[...]
+    out_txt[...] = txt[...]
 
 
 def solution(mesh):

time: 91.4 us -> 88.3 us (0.966)
  local copies, waits for them, and re-layouts: 1.86 us -> 0 us
  Pallas kernels: 86.1 us -> 84.9 us
    pallas_call x1, Pallas kernels: 86.1 us -> 83.6 us  [on_device(): pl.pallas_call(functools.partial(kernel, (nz, ny)), out_shape=(out, out),...]
    unnamed x4 -> x0, local copies, waits for them, and re-layouts: 1.86 us -> none
    pallas_call x0 -> x1, Pallas kernels: none -> 1.3 us  [on_device(): pl.pallas_call(hand_out, out_shape=(out, out), in_specs=[whole] * 2, out_...]
where the time goes in v4:
time: 88.3 us; the launch traced here: 88.1 us
  Pallas kernels  84.9 us (96%)
  between operations  3.22 us (4%)
    pallas_call x1, Pallas kernels, on_device(): pl.pallas_call(functools.partial(kernel, (nz, ny)), out_shape=(out, out),...  83.6 us

profile of v4, /device:TPU:1, one launch (start us, length us, event | category | flops | bytes accessed | tf_op | source)
XLA Modules:
  0.0 88.1 jit_solution(15479327021267682227)
XLA Ops:
  3.2 83.6 %learner_step.1 = (f32[8,128]{1,0:T(8,128)}, f32[8,128]{1,0:T(8,128)}) custom-call(bf16[512,1024]{1,0:T(8,128)(2,1)} %h_pool_img.1, bf16[512,1024]{1,0:T(8,128)(2,1)} %h_pool_txt.1, bf16[1024,128]{1,0:T(8,128)(2,1)} %h_w_img.1, bf16[1024,128]{1,0:T(8,128)(2,1)} %h_w_txt.1, s32[256]{0:T(256)} %h_sel.1, s32[1]{0:T(128)S(6)} %copy.14.cnt, f32[1]{0:T(128)S(6)} %copy.11.temper, ...), custom_call_target="tpu_custom_call" | custom-call | tf_op jit(solution)/shard_map/learner_step/pallas_call | solution.py:436
  86.8 1.3 %hand_out.1 = (f32[8,128]{1,0:T(8,128)}, f32[8,128]{1,0:T(8,128)}) custom-call(f32[8,128]{1,0:T(8,128)} %get-tuple-element.4.img, f32[8,128]{1,0:T(8,128)} %get-tuple-element.5.txt), custom_call_target="tpu_custom_call" | custom-call | tf_op jit(solution)/shard_map/hand_out/pallas_call | solution.py:450

commit v5 on v4

--- a/solution.py
+++ b/solution.py
@@ -42,10 +42,10 @@
     h_pool_img, h_pool_txt, h_w_img, h_w_txt, h_sel, cnt, temper, bias, loss_scale,
     out_img, out_txt,
     pool, w, sel,
-    feats, feats_t, proj, unit, norm, zbuf, pbuf, gimg, gtxt, wbuf, rs_out, rs_up, rs_dn,
-    rcore, sbuf, rxy, gp, gpr, gw, gwc, gx, gxr, gz, gzr,
+    feats, ft, fh, fh_send, proj, unit, norm, zbuf, pbuf, gimg, gtxt, wbuf, rs_out, rs_up, rs_dn,
+    rcore, sbuf, rxy, gp, gpr, gw, gx, gxr, gz, gzr,
     in_sem, y_sem, za_up, za_dn, xy_sem, cf_sem, zr_up, zr_dn, cr_sem, xr_sem, yb_sem,
-    fc_sem, fx_sem, fz_sem,
+    fh_sem, fx_sem, fz_sem,
 ):
     nz, ny = cfg
     row, y = lax.axis_index("rows"), lax.axis_index("tower")
@@ -89,6 +89,7 @@
         load.start()
     partners = [at(dx=dx, dy=dy) for dx, dy in order[1:]]
     partners += [at(dz=dz) for dz in [d for d in range(1, nz) if min(d, nz - d) <= NEAR_Z]] + [at(dc=1)]
+    partners += [at(dy=dy, dc=1) for dy in range(1, ny)]
     barrier = pltpu.get_barrier_semaphore()
     for there in partners:
         pl.semaphore_signal(
@@ -265,29 +266,33 @@
             gp[side * ny + k] = (
                 norm[side] * (part - unit[side * ny + k] * inner)
             ).astype(bf16)
-        for dy in (2, 1, 3):
-            if dy < ny:
-                send(gp.at[side * ny + (y + dy) % ny], gpr.at[side * ny + y],
-                     yb_sem.at[side, dy - 1], at(dy=dy))
-        gpr[side * ny + y] = gp[side * ny + y]
+        for dy in (2, 1, 3, 0):
+            for dc in range(NC):
+                if dy < ny and (dy or dc):
+                    send(gp.at[side * ny + (y + dy) % ny], gpr.at[(side * NC + dc) * ny + y],
+                         yb_sem.at[side, dc, dy], at(dy=dy, dc=dc))
+        gpr[side * NC * ny + y] = gp[side * ny + y]
 
     def weight_grad(side):
-        for dy in range(1, ny):
-            arrived(gpr.at[side * ny + (y - dy + ny) % ny], yb_sem.at[side, dy - 1])
-        grad = gpr[side * ny:(side + 1) * ny].reshape(ny * slots, col_w)
-        gw[side] = dot(feats_t[side], grad).reshape(gw.shape[1:])
-        send(gw.at[side, :, :, 1 - c], gwc.at[side], fc_sem.at[side], at(dc=1))
+        arrived(fh.at[side, 1], fh_sem.at[side])
+        total = None
+        for dc in range(NC):
+            first = (side * NC + dc) * ny
+            for dy in range(ny):
+                if dy or dc:
+                    arrived(gpr.at[first + (y - dy + ny) % ny], yb_sem.at[side, dc, dy])
+            part = dot(fh[side, dc], gpr[first:first + ny].reshape(ny * slots, col_w))
+            total = part if total is None else total + part
+        gw[side] = total.reshape(gw.shape[1:])
 
     far_first = sorted(range(nz), key=lambda d: -min(d, nz - d))
     per = nz // PARTS
 
     def over_x(side):
-        arrived(gwc.at[side], fc_sem.at[side])
         for part in range(PARTS):
             piece = pl.ds(part * per, per)
             for n in range(part * per, (part + 1) * per):
-                there = (z + far_first[n]) % nz
-                gx[side, n] = gw[side, there, :, c] + gwc[side, there]
+                gx[side, n] = gw[side, (z + far_first[n]) % nz]
             for dx in (2, 1, 3):
                 if dx < NX:
                     send(gx.at[side, piece, (x + dx) % NX], gxr.at[side, dx - 1, piece],
@@ -325,7 +330,10 @@
     embed(1)
     spread()
     for side in range(2):
-        feats_t[side] = feats[side].T
+        ft[...] = feats[side].T.astype(f32).reshape(ft.shape)
+        fh[side, 0] = ft[:, :, c].reshape(fh.shape[2:]).astype(bf16)
+        fh_send[side] = ft[:, :, 1 - c].reshape(fh.shape[2:]).astype(bf16)
+        send(fh_send.at[side], fh.at[side, 1], fh_sem.at[side], at(dc=1))
 
     for p in range(2, most_up // 2 + 2):
         ring_send(p)
@@ -393,7 +401,9 @@
         vmem((2, depth, col_w), bf16),
         vmem((list_len,), jnp.int32),
         vmem((2, list_len, depth), bf16),
-        vmem((2, depth, list_len), bf16),
+        vmem((nz, NX, NC, out_rows, list_len), f32),
+        vmem((2, NC, depth // NC, list_len), bf16),
+        vmem((2, depth // NC, list_len), bf16),
         vmem((2, list_len, col_w), f32),
         vmem((2 * ny, slots, col_w), f32),
         vmem((2, slots, 1), f32),
@@ -409,8 +419,7 @@
         vmem((chips, slots, emb_w), bf16),
         vmem((chips, slots, emb_w), bf16),
         vmem((2 * ny, slots, col_w), bf16),
-        vmem((2 * ny, slots, col_w), bf16),
-        vmem((2, nz, NX, NC, out_rows, col_w), f32),
+        vmem((2 * NC * ny, slots, col_w), bf16),
         vmem((2, nz, NX, out_rows, col_w), f32),
         vmem((2, nz, NX, out_rows, col_w), f32),
         vmem((2, NX - 1, nz, out_rows, col_w), f32),
@@ -426,7 +435,7 @@
         dma((most_up, ZCH, 2)),
         dma((chips // TILE, 2)),
         dma((chips - 1, 2)),
-        dma((2, ny - 1, 2)),
+        dma((2, NC, ny, 2)),
         dma((2, 2)),
         dma((2, NX - 1, PARTS, 2)),
         dma((2, nz - 1, 2)),

time: 88.3 us -> 87.5 us (level)
  Pallas kernels: 84.9 us -> 83.9 us
    pallas_call x1, Pallas kernels: 83.6 us -> 82.6 us  [on_device(): pl.pallas_call(functools.partial(kernel, (nz, ny)), out_shape=(out, out),...]
where the time goes in v5:
time: 87.5 us; the launch traced here: 87.1 us
  Pallas kernels  83.9 us (96%)
  between operations  3.22 us (4%)
    pallas_call x1, Pallas kernels, on_device(): pl.pallas_call(functools.partial(kernel, (nz, ny)), out_shape=(out, out),...  82.6 us

profile of v5, /device:TPU:1, one launch (start us, length us, event | category | flops | bytes accessed | tf_op | source)
XLA Modules:
  0.0 87.1 jit_solution(1273127974701158801)
XLA Ops:
  3.2 82.6 %learner_step.1 = (f32[8,128]{1,0:T(8,128)}, f32[8,128]{1,0:T(8,128)}) custom-call(bf16[512,1024]{1,0:T(8,128)(2,1)} %h_pool_img.1, bf16[512,1024]{1,0:T(8,128)(2,1)} %h_pool_txt.1, bf16[1024,128]{1,0:T(8,128)(2,1)} %h_w_img.1, bf16[1024,128]{1,0:T(8,128)(2,1)} %h_w_txt.1, s32[256]{0:T(256)} %h_sel.1, s32[1]{0:T(128)S(6)} %copy.14.cnt, f32[1]{0:T(128)S(6)} %copy.11.temper, ...), custom_call_target="tpu_custom_call" | custom-call | tf_op jit(solution)/shard_map/learner_step/pallas_call | solution.py:445
  85.8 1.3 %hand_out.1 = (f32[8,128]{1,0:T(8,128)}, f32[8,128]{1,0:T(8,128)}) custom-call(f32[8,128]{1,0:T(8,128)} %get-tuple-element.4.img, f32[8,128]{1,0:T(8,128)} %get-tuple-element.5.txt), custom_call_target="tpu_custom_call" | custom-call | tf_op jit(solution)/shard_map/hand_out/pallas_call | solution.py:459

commit v6 on v5

--- a/solution.py
+++ b/solution.py
@@ -352,30 +352,30 @@
     core_send(tiles - 1)
     done = 0
     for p in range(2, most_up // 2 + 1):
-        for t in range(done, min(done + 2, tiles)):
+        for t in range(done, min(done + 3, tiles)):
             plane_send(t)
-        done = min(done + 2, tiles)
+        done = min(done + 3, tiles)
         ring_sum(p)
     for t in range(done, tiles):
         plane_send(t)
     emb_i = zbuf[0].astype(f32)
     emb_t = pbuf[0, 0].astype(f32)
+    ring_sum(most_up // 2 + 1)
+    finish(0, gimg[0], emb_i, emb_t)
     for n in range(1, len(order)):
         arrived(rxy.at[n], xr_sem.at[n - 1])
     total = gtxt[0, 0]
     for n in range(1, len(order)):
         total = total + rxy[n].astype(f32)
     finish(1, total, emb_t, emb_i)
-    ring_sum(most_up // 2 + 1)
-    finish(0, gimg[0], emb_i, emb_t)
+    weight_grad(0)
+    over_x(0)
     weight_grad(1)
     over_x(1)
-    weight_grad(0)
-    over_x(0)
+    over_z(0)
     over_z(1)
-    over_z(0)
+    collect(0, out_img)
     collect(1, out_txt)
-    collect(0, out_img)
     for copy in sends:
         copy.wait_send()
 

time: 87.5 us -> 88.3 us (level); the launches traced: 87.1 us -> 86.7 us
  no operation moved by 1% of the time
where the time goes in v6:
time: 88.3 us; the launch traced here: 86.7 us
  Pallas kernels  83.5 us (95%)
  between operations  3.22 us (4%)
    pallas_call x1, Pallas kernels, on_device(): pl.pallas_call(functools.partial(kernel, (nz, ny)), out_shape=(out, out),...  82.2 us

profile of v6, /device:TPU:1, one launch (start us, length us, event | category | flops | bytes accessed | tf_op | source)
XLA Modules:
  0.0 86.7 jit_solution(12710240482553984655)
XLA Ops:
  3.2 82.2 %learner_step.1 = (f32[8,128]{1,0:T(8,128)}, f32[8,128]{1,0:T(8,128)}) custom-call(bf16[512,1024]{1,0:T(8,128)(2,1)} %h_pool_img.1, bf16[512,1024]{1,0:T(8,128)(2,1)} %h_pool_txt.1, bf16[1024,128]{1,0:T(8,128)(2,1)} %h_w_img.1, bf16[1024,128]{1,0:T(8,128)(2,1)} %h_w_txt.1, s32[256]{0:T(256)} %h_sel.1, s32[1]{0:T(128)S(6)} %copy.14.cnt, f32[1]{0:T(128)S(6)} %copy.11.temper, ...), custom_call_target="tpu_custom_call" | custom-call | tf_op jit(solution)/shard_map/learner_step/pallas_call | solution.py:445
  85.4 1.3 %hand_out.1 = (f32[8,128]{1,0:T(8,128)}, f32[8,128]{1,0:T(8,128)}) custom-call(f32[8,128]{1,0:T(8,128)} %get-tuple-element.4.img, f32[8,128]{1,0:T(8,128)} %get-tuple-element.5.txt), custom_call_target="tpu_custom_call" | custom-call | tf_op jit(solution)/shard_map/hand_out/pallas_call | solution.py:459
